TPU v7x, 128 devices: a whole 4x4x4 slice. The times are simulated.
128 devices in a mesh: ctx: 16 (over z_lo, y, core), fsdp: 8 (over z_hi, x).
Axes of the slice: x: 4, y: 4, z: 4 (z_hi: 2, z_lo: 2; z = z_hi * 2 + z_lo), core: 2. Of those that a mesh axis runs over, the one named last changes fastest.
Arguments:
- layer_input: bfloat16 [6144, 2048], P('ctx', 'fsdp'), may hold values from -6 to 6
- norm_gain: bfloat16 [2048], P('fsdp'), may hold values from 0.5 to 1.5
- norm_bias: bfloat16 [2048], P('fsdp'), may hold values from -1.75 to 1.75
- query_weight: bfloat16 [2048, 2048], P(None, 'fsdp'), may hold values from -0.125 to 0.125
- query_bias: bfloat16 [2048], P('fsdp'), may hold values from -1.75 to 1.75
- key_weight: bfloat16 [2048, 2048], P(None, 'fsdp'), may hold values from -0.125 to 0.125
- key_bias: bfloat16 [2048], P('fsdp'), may hold values from -1.75 to 1.75
- value_weight: bfloat16 [2048, 2048], P(None, 'fsdp'), may hold values from -0.125 to 0.125
- value_bias: bfloat16 [2048], P('fsdp'), may hold values from -0.3125 to 0.3125
- out_weight: bfloat16 [2048, 2048], P('fsdp'), may hold values from -2 to 2
- out_bias: bfloat16 [2048], P('fsdp'), may hold values from -3.5 to 3.5
- inner_weight: bfloat16 [2048, 8192], P(None, 'fsdp'), may hold values from -0.125 to 0.125
- inner_bias: bfloat16 [8192], P('fsdp'), may hold values from -1.75 to 1.75
- outer_weight: bfloat16 [8192, 2048], P('fsdp'), may hold values from -0.0625 to 0.0625
- outer_bias: bfloat16 [2048], P('fsdp'), may hold values from -3.5 to 3.5
- output_grad: bfloat16 [6144, 2048], P('ctx', 'fsdp'), may hold values from -6 to 6
- group_order: int32 [32], replicated, may hold values from 0 to 31, as said below
- sequence_ids: int32 [6144], replicated, may hold values from 0 to 4, as said below
Outputs:
- layer_output: bfloat16 [6144, 2048], P('ctx', 'fsdp')
- input_grad: float32 [6144, 2048], P('ctx', 'fsdp')
- norm_gain_grad: float32 [2048], P('fsdp')
- norm_bias_grad: float32 [2048], P('fsdp')
- query_weight_grad: float32 [2048, 2048], P(None, 'fsdp')
- query_bias_grad: float32 [2048], P('fsdp')
- key_weight_grad: float32 [2048, 2048], P(None, 'fsdp')
- key_bias_grad: float32 [2048], P('fsdp')
- value_weight_grad: float32 [2048, 2048], P(None, 'fsdp')
- value_bias_grad: float32 [2048], P('fsdp')
- out_weight_grad: float32 [2048, 2048], P('fsdp')
- out_bias_grad: float32 [2048], P('fsdp')
- inner_weight_grad: float32 [2048, 8192], P(None, 'fsdp')
- inner_bias_grad: float32 [8192], P('fsdp')
- outer_weight_grad: float32 [8192, 2048], P('fsdp')
- outer_bias_grad: float32 [2048], P('fsdp')
Inputs may be any that keep to these rules, and one draw needn't show every extreme that they name: `group_order`: slots 2 i and 2 i + 1 hold groups c and 31 - c for some c; every group is held once. `sequence_ids`: never falls along the positions; document 0 covers at least the first 3072 positions.
All inputs are finite; a program needn't handle non-finite values.
Results may differ from a plain program's by a relative error of at most 0.04.
Values may be sent and summed in bfloat16 or wider, within the bound.
A program may use at most 192 MiB of HBM per device.

v0:
```python
from functools import partial

import jax
import jax.numpy as jnp
from jax import lax
from jax.experimental import pallas as pl
from jax.experimental.pallas import tpu as pltpu
from jax.sharding import PartitionSpec as P

HEAD_DIM = 64
ROT = 32
GROUP = 192
GROUPS = 32
SEQ_LEN = 6144
DOCS = 5
EPS = 1e-05
MASKED = -1e30
FLOOR = -1e29
GELU_A = 0.7978845608028654
GELU_B = 0.044715
MESH = pl.DeviceIdType.MESH
BF16 = jnp.bfloat16
F32 = jnp.float32
ANY = pl.BlockSpec(memory_space=pl.ANY)
VMEM = pl.BlockSpec(memory_space=pltpu.VMEM)
SMEM = pl.BlockSpec(memory_space=pltpu.SMEM)
MIB = 2**20


class Group:
    def __init__(self, axis):
        ctx, fsdp = lax.axis_index("ctx"), lax.axis_index("fsdp")
        self.axis, self.ctx, self.fsdp = axis, ctx, fsdp
        self.core = lax.rem(ctx, 2)
        self.me = lax.div(ctx, 2) if axis == "ctx" else fsdp
        self.ring, self.pair = lax.rem(self.me, 4), lax.div(self.me, 4)

    def member(self, step, flip):
        pair = 1 - self.pair if flip else self.pair
        return pair * 4 + lax.rem(self.ring + (step + 4), 4)

    def device(self, step, flip):
        member = self.member(step, flip)
        if self.axis == "ctx":
            return (member * 2 + self.core, self.fsdp)
        return (self.ctx, member)

    def neighbours(self):
        return [self.device(1, 0), self.device(-1, 0), self.device(0, 1)]


def other_core(group):
    return (group.ctx + 1 - 2 * group.core, group.fsdp)


def barrier(devices):
    semaphore = pltpu.get_barrier_semaphore()
    for device in devices:
        pl.semaphore_signal(semaphore, inc=1, device_id=device, device_id_type=MESH)
    pl.semaphore_wait(semaphore, len(devices))


def remote(source, target, sems, slot, device):
    return pltpu.make_async_remote_copy(
        src_ref=source,
        dst_ref=target,
        send_sem=sems[0].at[slot],
        recv_sem=sems[1].at[slot],
        device_id=device,
        device_id_type=MESH,
    )


GATHER = (
    (1, 0, (0, 0), 0, 2, None),
    (-1, 0, (0, 0), 0, 2, None),
    (0, 1, (0, 0), 2, 4, None),
    (1, 0, (0, 0), 2, 4, None),
    (-1, 0, (0, 0), 2, 4, None),
    (0, 1, (0, 0), 0, 2, None),
    (1, 0, (-1, 0), 0, 1, 0),
    (-1, 0, (1, 0), 1, 2, 1),
    (0, 1, (-1, 0), 0, 2, 0),
    (0, 1, (1, 0), 0, 2, 1),
    (0, 1, (2, 0), 0, 1, 6),
    (0, 1, (2, 0), 1, 2, 7),
    (1, 0, (0, 1), 2, 4, 2),
    (-1, 0, (0, 1), 2, 4, 2),
    (1, 0, (-1, 0), 2, 3, 3),
    (-1, 0, (1, 0), 3, 4, 4),
    (1, 0, (-1, 1), 2, 3, 12),
    (-1, 0, (1, 1), 3, 4, 13),
)
GATHER_ORDER = (0, 1, 2, 3, 4, 6, 7, 12, 13, 5, 8, 14, 15, 9, 10, 16, 17, 11)
GATHER_SLOTS = len(GATHER)


def gather(group, view, sems, arrived=None, own=None):
    started = []

    def start(slot):
        step, flip, block, a, b, _ = GATHER[slot]

        def copy():
            ref = view(group.member(*block), a, b)
            source = own(a, b) if own and block == (0, 0) else ref
            return remote(source, ref, sems, slot, group.device(step, flip))

        copy().start()
        started.append(copy)

    for slot in range(GATHER_SLOTS):
        if GATHER[slot][5] is None:
            start(slot)
    if arrived:
        arrived((0, 0), 0, 4)
    for slot in GATHER_ORDER:
        step, flip, block, a, b, _ = GATHER[slot]
        yield
        source = (block[0] - step, block[1] ^ flip)
        ref = view(group.member(*source), a, b)
        remote(ref, ref, sems, slot, group.device(step, flip)).wait_recv()
        for later in range(GATHER_SLOTS):
            if GATHER[later][5] == slot:
                start(later)
        if arrived:
            arrived(source, a, b)
    for copy in started:
        copy().wait_send()


SCATTER_SLOTS = 23
HOLD = 7


def add_into(target, *sources):
    total = target[...].astype(F32)
    for source in sources:
        total = total + source[...].astype(F32)
    target[...] = total.astype(target.dtype)


def scatter(group, part, quarters, hold, result, sems, pair_first=True, prepare=None):
    started = []

    def held(k, a, b):
        return quarters(hold.at[k], a, b)

    def start(slot, source, step, flip, k, a, b):
        def copy():
            return remote(source(), held(k, a, b), sems, slot, group.device(step, flip))

        copy().start()
        started.append(copy)

    prepared = []

    def ready(block):
        if prepare and block not in prepared:
            prepared.append(block)
            prepare(*block)

    def send_part(slot, block, step, flip, k, a, b):
        ready(block)
        start(slot, lambda: part(*block, a, b), step, flip, k, a, b)

    def send_held(slot, source, step, flip, k, a, b):
        start(slot, lambda: held(source, a, b), step, flip, k, a, b)

    def wait(slot, k, a, b):
        ref = held(k, a, b)
        remote(ref, ref, sems, slot, group.device(0, 1)).wait_recv()

    if pair_first:
        send_part(0, (2, 1), 0, 1, 0, 0, 2)
    send_part(10, (2, 1), 1, 0, 0, 2, 3)
    send_part(11, (2, 1), -1, 0, 0, 3, 4)
    if pair_first:
        send_part(1, (1, 1), 0, 1, 1, 0, 2)
        send_part(2, (-1, 1), 0, 1, 2, 0, 2)
    send_part(16, (2, 0), 1, 0, 3, 2, 3)
    send_part(17, (2, 0), -1, 0, 3, 3, 4)
    send_part(12, (1, 1), 1, 0, 1, 3, 4)
    send_part(13, (-1, 1), -1, 0, 2, 2, 3)
    send_part(18, (1, 0), 1, 0, 4, 3, 4)
    send_part(19, (-1, 0), -1, 0, 5, 2, 3)
    if pair_first:
        send_part(3, (0, 1), 0, 1, 3, 0, 2)
    ready((0, 1))
    ready((0, 0))
    yield
    wait(10, 0, 2, 3)
    add_into(held(0, 2, 3), part(1, 1, 2, 3))
    send_held(14, 0, 1, 0, 1, 2, 3)
    wait(11, 0, 3, 4)
    add_into(held(0, 3, 4), part(-1, 1, 3, 4))
    send_held(15, 0, -1, 0, 2, 3, 4)
    if pair_first:
        yield
        wait(0, 0, 0, 2)
        add_into(held(0, 0, 2), part(2, 0, 0, 2))
        send_held(4, 0, 1, 0, 4, 0, 1)
        send_held(5, 0, -1, 0, 4, 1, 2)
    yield
    wait(16, 3, 2, 3)
    add_into(held(3, 2, 3), part(1, 0, 2, 3))
    send_held(20, 3, 1, 0, 4, 2, 3)
    wait(17, 3, 3, 4)
    add_into(held(3, 3, 4), part(-1, 0, 3, 4))
    send_held(21, 3, -1, 0, 5, 3, 4)
    if pair_first:
        yield
        wait(1, 1, 0, 2)
        add_into(held(1, 0, 2), part(1, 0, 0, 2))
        send_held(6, 1, 1, 0, 5, 1, 2)
    yield
    wait(12, 1, 3, 4)
    wait(14, 1, 2, 3)
    wait(13, 2, 2, 3)
    wait(15, 2, 3, 4)
    add_into(held(1, 2, 4), held(2, 2, 4), part(0, 1, 2, 4))
    send_held(22, 1, 0, 1, 6, 2, 4)
    if pair_first:
        yield
        wait(2, 2, 0, 2)
        add_into(held(2, 0, 2), part(-1, 0, 0, 2))
        send_held(8, 2, -1, 0, 6, 0, 1)
        yield
        wait(4, 4, 0, 1)
        add_into(held(1, 0, 1), held(4, 0, 1))
        send_held(7, 1, 1, 0, 5, 0, 1)
        wait(5, 4, 1, 2)
        add_into(held(2, 1, 2), held(4, 1, 2))
        send_held(9, 2, -1, 0, 6, 1, 2)
        yield
        wait(3, 3, 0, 2)
        wait(6, 5, 1, 2)
        wait(8, 6, 0, 1)
        wait(7, 5, 0, 1)
        wait(9, 6, 1, 2)
        result(0, 2, [part(0, 0, 0, 2), held(3, 0, 2), held(5, 0, 2), held(6, 0, 2)])
    yield
    wait(18, 4, 3, 4)
    wait(20, 4, 2, 3)
    wait(19, 5, 2, 3)
    wait(21, 5, 3, 4)
    wait(22, 6, 2, 4)
    result(2, 4, [part(0, 0, 2, 4), held(4, 2, 4), held(5, 2, 4), held(6, 2, 4)])
    for copy in started:
        copy().wait_send()


def total_of(refs):
    total = refs[0][...].astype(F32)
    for ref in refs[1:]:
        total = total + ref[...].astype(F32)
    return total


def drain(*programs):
    programs = list(programs)
    while programs:
        programs = [p for p in programs if next(p, "end") != "end"]


def pairs(count):
    return [pltpu.SemaphoreType.DMA((count,)), pltpu.SemaphoreType.DMA((count,))]


def params(collective_id, mib):
    return pltpu.CompilerParams(
        collective_id=collective_id, has_side_effects=True, vmem_limit_bytes=mib * MIB
    )


ROW_CUTS = (0, 96, 192, 288, 400)


TILE = 2 * GROUP
TILES = SEQ_LEN // TILE
ITEMS = TILES + 1
KEYS, VALUES = slice(0, 128), slice(128, 256)
NT = (((1,), (1,)), ((), ()))
TN = (((0,), (0,)), ((), ()))


def dot(a, b, dims=(((1,), (0,)), ((), ()))):
    return lax.dot_general(a, b, dims, preferred_element_type=F32)


class Steps:
    def __init__(self, *programs):
        self.programs = list(programs)

    def take(self, count=1):
        for _ in range(count):
            self.programs = [p for p in self.programs if next(p, "end") != "end"]

    def at(self, j, plan):
        for iteration, count in plan:
            pl.when(j == iteration)(partial(self.take, count))

    def finish(self):
        drain(*self.programs)


class Copies:
    def __init__(self, sems):
        self.sems, self.made = sems, []

    def start(self, source, target):
        slot = len(self.made)

        def copy():
            return pltpu.make_async_copy(source(), target(), self.sems.at[slot])

        copy().start()
        self.made.append(copy)
        return slot

    def wait(self, *slots):
        for slot in slots:
            self.made[slot]().wait()
            self.made[slot] = None

    def finish(self):
        self.wait(*[slot for slot, copy in enumerate(self.made) if copy])


def chunk_of(i, size):
    return pl.ds(pl.multiple_of(i * size, size), size)


def turned(values, cosine, sine):
    lane = lax.rem(lax.broadcasted_iota(jnp.int32, (1, 128), 1), HEAD_DIM)
    swapped = jnp.where(lane < ROT // 2, -pltpu.roll(values, 128 - ROT // 2, 1), pltpu.roll(values, ROT // 2, 1))
    return values * cosine + swapped * sine


def cut_rows(ref, a, b):
    step = ref.shape[0] // 4
    return ref.at[pl.ds(step * a, step * (b - a)), :]


def rows_scatter(group, part_ref, out, arriving, hold, sems):
    cs, cr, send, recv = sems
    core, partner = group.core, other_core(group)

    def exchange():
        return remote(part_ref.at[1 - core], arriving, (cs, cr), 0, partner)

    exchange().start()
    yield
    exchange().wait()

    def one(i, carry):
        rows = pl.ds(pl.multiple_of(i * 32, 32), 32)
        arriving[rows, :] = (arriving[rows, :].astype(F32) + part_ref[core, rows, :].astype(F32)).astype(BF16)
        return carry

    lax.fori_loop(0, arriving.shape[0] // 32, one, 0)
    width, size = out.shape[1], out.shape[0] // 2

    def cut(ref, a, b):
        return ref.at[pl.ds(size * (a - 2), size * (b - a)), :]

    def part(step, flip, a, b):
        columns = pl.ds(pl.multiple_of(group.member(step, flip) * width, width), width)
        return arriving.at[pl.ds(size * (a - 2), size * (b - a)), columns]

    def result(a, b, refs):
        target = cut(out, a, b)
        target[...] = total_of(refs)

    yield from scatter(group, part, cut, hold, result, (send, recv), pair_first=False)


def peers(axis):
    ctx, fsdp = lax.axis_index("ctx"), lax.axis_index("fsdp")
    count = lax.axis_size(axis)
    if axis == "ctx":
        return [(lax.rem(ctx + offset, count), fsdp) for offset in range(1, count)]
    return [(ctx, lax.rem(fsdp + offset, count)) for offset in range(1, count)]


def sum_small(x_ref, out, hold, sems, devices):
    def copy(i):
        return remote(x_ref, hold.at[i], sems, i, devices[i])

    for i in range(len(devices)):
        copy(i).start()
    yield
    total = x_ref[...]
    for i in range(len(devices)):
        copy(i).wait_recv()
        total = total + hold[i]
    out[...] = total
    for i in range(len(devices)):
        copy(i).wait_send()


def reduce_one(group, source, target, hold, sems):
    rs, rr, gs, gr, cs, cr, ls = sems
    core, partner = group.core, other_core(group)
    rows, width = source.shape[0] // 8, source.shape[1]
    by_rows = rows % 64 == 0

    def quarters(ref, a, b):
        if by_rows:
            return ref.at[pl.ds(rows // 4 * a, rows // 4 * (b - a)), :]
        return ref.at[:, pl.ds(width // 4 * a, width // 4 * (b - a))]

    def part(step, flip, a, b):
        return quarters(source.at[chunk_of(group.member(step, flip), rows), :], a, b)

    def view(member, a, b):
        return quarters(target(core).at[chunk_of(member, rows), :], a, b)

    def own(a, b):
        return quarters(hold.at[HOLD - 1], a, b)

    def result(a, b, terms):
        place = own(a, b)
        place[...] = total_of(terms).astype(BF16)

    def keep():
        return pltpu.make_async_copy(own(0, 4), view(group.me, 0, 4), ls.at[0])

    copies = []

    def arrived(block, a, b):
        slot = len(copies)

        def copy():
            ref = view(group.member(*block), a, b)
            return remote(own(a, b) if block == (0, 0) else ref, ref, (cs, cr), slot, partner)

        copy().start()
        copies.append(copy)

    yield from scatter(group, part, quarters, hold, result, (rs, rr))
    keep().start()
    yield from gather(group, view, (gs, gr), arrived, own=own)
    yield
    keep().wait()
    for copy in copies:
        copy().wait()


def reduce_scratch(shape):
    return pltpu.VMEM((HOLD, shape[0] // 8, shape[1]), BF16)


def reduce_sems():
    return pairs(SCATTER_SLOTS) + pairs(GATHER_SLOTS) + pairs(GATHER_SLOTS + 1) + [pltpu.SemaphoreType.DMA((1,))]


STATES = 11


def state_of(j):
    late = lax.div(j + 7, 16)
    return j * (1 - late) + (9 + lax.rem(j, 2)) * late


FORWARD_PLAN = ((1, 1), (3, 1), (4, 1), (8, 1), (11, 1), (13, 1), (14, 1))
BACKWARD_PLAN = ((0, 1), (2, 1), (8, 3), (12, 2), (14, 2), (16, 2))
BRANCH_PLAN = ((2, 1), (5, 1), (8, 1), (12, 1))
OUT_PLAN = ((4, 2), (6, 2), (9, 2), (11, 1), (13, 2), (15, 5))
ROWS, LAST, EARLY, WEIGHTS, OUT = range(5)
TAIL_PLAN = (
    (ROWS, 1), (EARLY, 3), (EARLY, 2), (LAST, 3), (EARLY, 2), (LAST, 1), (ROWS, 1), (LAST, 1), (EARLY, 1), (LAST, 2), (ROWS, 1), (EARLY, 1),
    (LAST, 2), (ROWS, 1), (EARLY, 5), (LAST, 5), (EARLY, 4), (LAST, 4), (ROWS, 1),
)


def layer_kernel(
    order_ref, ids_ref, x_ref, dy_ref, vectors_ref, wq, wk, wv, wo, wi, wu,
    layer_out, input_out, vec_out, q_out, k_out, v_out, out_out, inner_out, outer_out,
    x_all, dy_all, normed, qkv_w, o_w, i_w, u_w, kv_all, inner, act, act_t, grad, ff, ffn, inner_part, outer_part, out_part,
    cos_ref, sin_ref, q_ref, cotangent_ref, begin_ref, unit_ref, inv_ref, inner_sum, slot_of,
    state_max, state_sum, state_acc, dkv_items, lse_ref, delta_ref, att_ref, dq_ref,
    arriving, branch_hold, sum_ref, arriving_back, back_hold, local_ref, inner_hold, outer_hold, q_hold, k_hold, v_hold, out_hold, keys_hold, own, pre,
    stats, stats_hold, stats_sum, vec, vec_hold,
    *sems,
):
    across, along = Group("ctx"), Group("fsdp")
    core, chip, fsdp, partner = across.core, across.me, along.me, other_core(across)
    rows, width = dy_ref.shape
    sems = list(sems)

    def sems_for(count):
        taken = sems[:count]
        del sems[:count]
        return taken

    xs, ds, ks, cs = sems_for(2), sems_for(2), sems_for(2), sems_for(2)
    copies = Copies(sems_for(1)[0])
    x_cuts = (0, 96, 192, 288, x_all.shape[0])

    def x_view(member, a, b):
        return x_all.at[pl.ds(x_cuts[a], x_cuts[b] - x_cuts[a]), chunk_of(member, width)]

    def dy_view(member, a, b):
        return dy_all.at[core, pl.ds(rows // 4 * a, rows // 4 * (b - a)), chunk_of(member, width)]

    copies.start(lambda: x_ref, lambda: x_all.at[pl.ds(0, rows), chunk_of(fsdp, width)])
    copies.start(lambda: dy_ref, lambda: dy_view(fsdp, 0, 4))
    for i, ref in enumerate((wq, wk, wv)):
        copies.start(lambda ref=ref: ref.at[:, chunk_of(core, 128)], lambda i=i: qkv_w.at[:, pl.ds(128 * i, 128)])
    copies.start(lambda: wi.at[:, chunk_of(core, 512)], lambda: i_w)
    copies.start(lambda: wu.at[chunk_of(core, 512), :], lambda: u_w)
    copies.start(lambda: wo.at[chunk_of(core, 128), :], lambda: o_w)
    def vector(i):
        return vectors_ref[:, 256 * i : 256 * i + 256]

    extra = jnp.concatenate([vector(0), vector(1), jnp.zeros((14, width), F32)], axis=0)
    x_all[rows:, chunk_of(fsdp, width)] = extra.astype(BF16)
    barrier(peers("ctx") + peers("fsdp"))
    copies.wait(0, 1)
    x_steps = Steps(gather(along, x_view, xs))
    x_steps.take()
    dy_steps = Steps(gather(along, dy_view, ds))

    lane = lax.rem(lax.broadcasted_iota(jnp.int32, (1, 128), 1), HEAD_DIM)
    left = lax.broadcasted_iota(jnp.int32, (1, 128), 1) < HEAD_DIM
    freqs = jnp.zeros((1, 128), F32)
    for i in range(ROT):
        freqs = jnp.where(lane == i, 10000.0 ** (-2.0 * (i % (ROT // 2)) / ROT), freqs)
    for slot in range(4):
        group = order_ref[chip * 4 + slot]
        position = (group * GROUP + lax.broadcasted_iota(jnp.int32, (GROUP, 128), 0)).astype(F32)
        angles = position * freqs
        place = slice(GROUP * slot, GROUP * slot + GROUP)
        cos_ref[place, :] = jnp.cos(angles)
        sin_ref[place, :] = jnp.sin(angles)
        column = lax.broadcasted_iota(jnp.int32, (1, TILE), 1)
        column = group * GROUP + jnp.where(column < GROUP, column, column - GROUP)
        begin = jnp.zeros((1, TILE), jnp.int32)
        for doc in range(1, DOCS):
            before = jnp.sum(jnp.where(ids_ref[...] < doc, 1, 0), axis=0, keepdims=True)
            before = jnp.sum(before, axis=1, keepdims=True)
            begin = jnp.where(before <= column, before, begin)
        begin_ref[slot] = begin

    def find(group, carry):
        place = 0
        for slot in range(1, GROUPS):
            apart = order_ref[slot] - group
            place = place + slot * (1 - jnp.minimum(apart * apart, 1))
        slot_of[group] = jnp.minimum(place, GROUPS - 1)
        return carry

    lax.fori_loop(0, GROUPS, find, 0)

    x_steps.take(9)
    dy_steps.take()
    x_steps.finish()
    gain, shift = x_all[rows : rows + 1, :].astype(F32), x_all[rows + 1 : rows + 2, :].astype(F32)

    def exchange(ref, i):
        half = ref.at[core, pl.ds(GROUP * i, GROUP), :]
        return remote(half, half, cs, 2 * (ref is dy_all) + i, partner)

    def norm(i, carry):
        place = chunk_of(i, 32)
        values = x_all[place, :].astype(F32)
        mean = jnp.mean(values, axis=1, keepdims=True)
        centered = values - mean
        inv = lax.rsqrt(jnp.mean(centered * centered, axis=1, keepdims=True) + EPS)
        normed[core, place, :] = (centered * inv * gain + shift).astype(BF16)
        unit_ref[place, :] = (x_all[place, chunk_of(fsdp, width)].astype(F32) - mean) * inv
        inv_ref[place, :] = inv
        return carry

    for i in range(2):
        lax.fori_loop(GROUP // 32 * i, GROUP // 32 * (i + 1), norm, 0)
        exchange(normed, i).start()
    copies.wait(2, 3, 4)
    dy_steps.take(3)

    def project(of):
        pre_rows = dot(normed[of], qkv_w[...])
        bias = [vectors_ref[:, pl.ds(pl.multiple_of(512 + 256 * i + 128 * core, 128), 128)] for i in range(3)]
        for half in range(2):
            slot, part_rows = 2 * of + half, slice(GROUP * half, GROUP * half + GROUP)
            cosine, sine = cos_ref[chunk_of(slot, GROUP), :], sin_ref[chunk_of(slot, GROUP), :]
            queries = turned(pre_rows[part_rows, :128] + bias[0], cosine, sine).astype(BF16)
            q_ref[slot] = (queries.astype(F32) * HEAD_DIM ** (-0.5)).astype(BF16)
            kv_all[4 * chip + slot, :, :128] = turned(pre_rows[part_rows, 128:256] + bias[1], cosine, sine).astype(BF16)
            kv_all[4 * chip + slot, :, 128:] = (pre_rows[part_rows, 256:] + bias[2]).astype(BF16)

    def both_cores(one, ref):
        def here():
            for i in range(2):
                exchange(ref, i).wait()

        def loop(i, carry):
            pl.when(i == 1)(here)
            one(lax.rem(core + i, 2))
            return carry

        lax.fori_loop(0, 2, loop, 0)

    both_cores(project, normed)

    def kv_view(member, a, b):
        return kv_all.at[pl.ds(4 * member + a, b - a)]

    kv_steps = Steps(gather(across, kv_view, ks))
    kv_steps.take()
    dy_steps.take(6)
    copies.wait(5, 6, 7)

    inner_bias = vectors_ref[:, pl.ds(pl.multiple_of(1792 + 512 * core, 128), 512)]

    def feed(of, carry):
        value = dot(normed[of], i_w[...]) + inner_bias
        inner[chunk_of(of, rows), :] = value
        curve = jnp.tanh(GELU_A * (value + GELU_B * value * value * value))
        act[chunk_of(of, rows), :] = (0.5 * value * (1.0 + curve)).astype(BF16)
        return carry

    lax.fori_loop(0, 2, feed, 0)
    dy_steps.take(4)
    kv_steps.take(3)

    def feed_out(i, carry):
        block = chunk_of(i, 256)
        ff[:, :, block] = dot(act[...], u_w[:, block]).astype(BF16).reshape(2, rows, 256)
        return carry

    lax.fori_loop(0, 8, feed_out, 0)
    act_t[...] = act[...].T
    dy_steps.finish()
    for i in range(2):
        exchange(dy_all, i).start()
    kv_steps.take(2)
    inner_sum[...] = jnp.zeros_like(inner_sum)

    def gradients(of):
        dy_rows = dy_all[of]
        ag = dot(dy_rows, o_w[...], NT).astype(BF16)
        cotangent_ref[2 * of], cotangent_ref[2 * of + 1] = ag[:GROUP], ag[GROUP:]
        value = inner[chunk_of(of, rows), :]
        square = value * value
        curve = jnp.tanh(GELU_A * (value + GELU_B * square * value))
        slope = 0.5 * (1.0 + curve) + 0.5 * value * (1.0 - curve * curve) * (GELU_A * (1.0 + 3.0 * GELU_B * square))
        out = (dot(dy_rows, u_w[...], NT) * slope).astype(BF16)
        grad[chunk_of(of, rows), :] = out
        inner_sum[...] += jnp.sum(out.astype(F32), axis=0, keepdims=True)

    both_cores(gradients, dy_all)
    kv_steps.take(2)

    def outer_weights(i, carry):
        block = chunk_of(i, 256)
        outer_part[:, block] = dot(act_t[...], dy_all[:, :, block].reshape(2 * rows, 256)).astype(BF16)
        return carry

    lax.fori_loop(0, 8, outer_weights, 0)
    outer_program = reduce_one(across, outer_part, lambda c: outer_out.at[c], outer_hold, sems_for(7))
    inner_program = reduce_one(across, inner_part, lambda c: inner_out.at[:, chunk_of(c, 512)], inner_hold, sems_for(7))
    kv_steps.take(2)
    next(outer_program)

    def inner_weights(i, carry):
        block = chunk_of(i, 256)
        inner_part[block, :] = dot(normed[:, :, block].reshape(2 * rows, 256), grad[...], TN).astype(BF16)
        return carry

    lax.fori_loop(0, 8, inner_weights, 0)
    kv_steps.take(2)
    next(inner_program)

    kv_steps.finish()
    weights_steps = Steps(outer_program, inner_program)

    def bit(number):
        return jnp.minimum(jnp.maximum(number, 0), 1)

    def pair_facts(p):
        g0, g1 = order_ref[4 * chip + 2 * p], order_ref[4 * chip + 2 * p + 1]
        low, high = jnp.minimum(g0, g1), jnp.maximum(g0, g1)
        return low, high, bit(g0 - g1), lax.div(low, 2) + 1

    key_row = lax.broadcasted_iota(jnp.int32, (TILE, TILE), 0)
    column = lax.broadcasted_iota(jnp.int32, (1, TILE), 1)
    query_row = jnp.where(column < GROUP, column, column - GROUP)

    def item_facts(p, j):
        low, high, low_slot, count = pair_facts(p)
        second = bit(j - count + 1)
        tile = second * TILES + (1 - second) * (count - 1) - j
        slot = 2 * p + second * (1 - low_slot) + (1 - second) * low_slot
        position = (second * high + (1 - second) * low) * GROUP
        last = query_row + (position - tile * TILE)
        begin = begin_ref[slot] - tile * TILE
        allowed = (key_row <= last) & (key_row >= begin)
        keep = bit(j * (j - count) * (j - count)).astype(F32)
        return tile, slot, allowed, keep

    def keys_of(tile, lanes):
        return jnp.concatenate([kv_all[slot_of[2 * tile], :, lanes], kv_all[slot_of[2 * tile + 1], :, lanes]], axis=0)

    def stacked(rows):
        zero = jnp.zeros_like(rows)
        return jnp.concatenate([jnp.where(left, rows, zero), jnp.where(left, zero, rows)], axis=0)

    def unstacked(columns):
        rows = columns.T
        return jnp.where(left, rows[:GROUP], rows[GROUP:])

    def final_item(p, i):
        low, high, low_slot, count = pair_facts(p)
        is_low = low_slot if i else 1 - low_slot
        return count * is_low + 10 * (1 - is_low)

    for p in range(2):
        state_max[p, 0] = jnp.full((1, TILE), FLOOR, F32)
        state_sum[p, 0] = jnp.zeros((1, TILE), F32)
        state_acc[p, 0] = jnp.zeros((128, TILE), F32)

    def forward(j, carry):
        weights_steps.at(j, FORWARD_PLAN)
        now, after = state_of(j), state_of(j + 1)
        for p in range(2):
            tile, slot, allowed, keep = item_facts(p, j)
            scores = jnp.where(allowed, dot(keys_of(tile, KEYS), stacked(q_ref[slot]), NT), MASKED)
            old_max = state_max[p, now] * keep + FLOOR * (1.0 - keep)
            new_max = jnp.maximum(old_max, jnp.max(scores, axis=0, keepdims=True))
            weights = jnp.exp(scores - new_max)
            factor = jnp.exp(old_max - new_max)
            state_max[p, after] = new_max
            state_sum[p, after] = state_sum[p, now] * factor + jnp.sum(weights, axis=0, keepdims=True)
            state_acc[p, after] = state_acc[p, now] * factor + dot(keys_of(tile, VALUES), weights.astype(BF16), TN)
        return carry

    lax.fori_loop(0, ITEMS, forward, 0)

    for p in range(2):
        for i in range(2):
            item = final_item(p, i)
            slot = 2 * p + i
            total = state_sum[p, item]
            out = state_acc[p, item] / total
            lse_ref[slot] = state_max[p, item] + jnp.log(total)
            cotangent = stacked(cotangent_ref[slot].astype(F32)).T
            delta_ref[slot] = jnp.sum(cotangent * out, axis=0, keepdims=True)
            att_ref[slot] = unstacked(out).astype(BF16)

    def branches(i, carry):
        block = chunk_of(i, 256)
        attended = dot(att_ref[...].reshape(2 * rows, 128), o_w[:, block]).reshape(2, rows, 256)
        ff[:, :, block] = (ff[:, :, block].astype(F32) + attended).astype(BF16)
        return carry

    lax.fori_loop(0, 8, branches, 0)
    branch_steps = Steps(rows_scatter(along, ff, sum_ref, arriving, branch_hold, sems_for(4)))
    branch_steps.take()

    def out_weights(i, carry):
        block = chunk_of(i, 256)
        out_part[:, block] = dot(att_ref[...].reshape(2 * rows, 128), dy_all[:, :, block].reshape(2 * rows, 256), TN).astype(BF16)
        return carry

    lax.fori_loop(0, 8, out_weights, 0)
    out_steps = Steps(reduce_one(across, out_part, lambda c: out_out.at[c], out_hold, sems_for(7)))
    out_steps.take()

    for p in range(2):
        state_acc[p, 0] = jnp.zeros((128, TILE), F32)

    def backward(j, carry):
        weights_steps.at(j, BACKWARD_PLAN)
        branch_steps.at(j, BRANCH_PLAN)
        out_steps.at(j, OUT_PLAN)
        now, after = state_of(j), state_of(j + 1)
        for p in range(2):
            tile, slot, allowed, keep = item_facts(p, j)
            queries, cotangent = stacked(q_ref[slot]), stacked(cotangent_ref[slot])
            scores = dot(keys_of(tile, KEYS), queries, NT)
            probs = jnp.where(allowed, jnp.exp(scores - lse_ref[slot]), 0.0)
            prob_grad = dot(keys_of(tile, VALUES), cotangent, NT)
            score_grad = (probs * (prob_grad - delta_ref[slot])).astype(BF16)
            state_acc[p, after] = state_acc[p, now] * keep + dot(keys_of(tile, KEYS), score_grad, TN)
            key_grad = dot(score_grad, queries).astype(BF16)
            value_grad = dot(probs.astype(BF16), cotangent).astype(BF16)
            for half in range(2):
                rows = slice(GROUP * half, GROUP * half + GROUP)
                dkv_items[p, j, half, :, :128] = key_grad[rows]
                dkv_items[p, j, half, :, 128:] = value_grad[rows]
        return carry

    lax.fori_loop(0, ITEMS, backward, 0)

    for p in range(2):
        for i in range(2):
            dq_ref[2 * p + i] = unstacked(state_acc[p, final_item(p, i)])

    counts = [pair_facts(p)[3] for p in range(2)]

    def collect(s, carry):
        group = order_ref[s]
        tile, half = lax.div(group, 2), lax.rem(group, 2)
        total = jnp.zeros((GROUP, 256), F32)
        for p in range(2):
            low_item = dkv_items[p, jnp.maximum(counts[p] - 1 - tile, 0), half].astype(F32)
            high_item = dkv_items[p, jnp.maximum(TILES - tile, counts[p]), half].astype(F32)
            total = total + low_item * bit(counts[p] - tile).astype(F32)
            total = total + high_item * bit(TILES - tile - counts[p] + 1).astype(F32)
        kv_all[s] = total.astype(BF16)
        return carry

    def collect_member(step, flip):
        start = 4 * across.member(step, flip)
        lax.fori_loop(start, start + 4, collect, 0)

    def part(step, flip, a, b):
        return kv_all.at[pl.ds(4 * across.member(step, flip) + a, b - a)]

    def cut_groups(ref, a, b):
        return ref.at[pl.ds(a, b - a)]

    def result(a, b, refs):
        own[a:b] = total_of(refs)

    keys_steps = Steps(scatter(across, part, cut_groups, keys_hold, result, sems_for(2), prepare=collect_member))
    keys_steps.take()
    branch_steps.finish()
    layer_sum = x_all[:rows, chunk_of(fsdp, width)].astype(F32) + sum_ref[...]
    layer_out[...] = (layer_sum + vector(5) + vector(6)).astype(BF16)
    for slot in range(4):
        place = slice(GROUP * slot, GROUP * slot + GROUP)
        turned_back = turned(dq_ref[slot] * HEAD_DIM ** (-0.5), cos_ref[place, :], -sin_ref[place, :])
        pre[place, :128] = turned_back.astype(BF16)
    q_part, k_part, v_part = [inner_part.at[:, pl.ds(128 * i, 128)] for i in range(3)]

    def query_weights(i, carry):
        block = chunk_of(i, 256)
        q_part[block, :] = dot(normed[:, :, block].reshape(2 * rows, 256), pre[:, :128], TN).astype(BF16)
        return carry

    lax.fori_loop(0, 8, query_weights, 0)
    keys_steps.take()

    early_steps = Steps(reduce_one(across, q_part, lambda c: q_out.at[:, chunk_of(c, 128)], q_hold, sems_for(7)))
    keys_steps.take()
    early_steps.take()
    def feed_back(i, carry):
        block = chunk_of(i, 256)
        ffn[:, :, block] = dot(grad[...], i_w[block, :], NT).astype(BF16).reshape(2, rows, 256)
        return carry

    lax.fori_loop(0, 8, feed_back, 0)
    weights_steps.take(2)
    keys_steps.take(2)
    weights_steps.take(2)
    keys_steps.take(2)
    weights_steps.take(2)
    keys_steps.finish()
    for slot in range(4):
        place = slice(GROUP * slot, GROUP * slot + GROUP)
        turned_back = turned(own[slot, :, :128], cos_ref[place, :], -sin_ref[place, :])
        pre[place, 128:256] = turned_back.astype(BF16)
        pre[place, 256:] = own[slot, :, 128:].astype(BF16)

    def key_weights(i, carry):
        block = chunk_of(i, 256)
        total = dot(normed[:, :, block].reshape(2 * rows, 256), pre[:, 128:], TN).astype(BF16)
        k_part[block, :] = total[:, :128]
        v_part[block, :] = total[:, 128:]
        return carry

    def normed_grad(of):
        def one(i, carry):
            part_rows, columns = chunk_of(lax.div(i, 4), GROUP), chunk_of(lax.rem(i, 4), 512)
            from_rows = chunk_of(2 * of + lax.div(i, 4), GROUP)
            total = ffn[of, part_rows, columns].astype(F32) + dot(pre[from_rows, :], qkv_w[columns, :], NT)
            ffn[of, part_rows, columns] = total.astype(BF16)
            return carry

        lax.fori_loop(0, 8, one, 0)

    normed_grad(1 - core)
    rows_steps = Steps(rows_scatter(along, ffn, local_ref, arriving_back, back_hold, sems_for(4)))
    rows_steps.take()
    lax.fori_loop(0, 8, key_weights, 0)
    last_steps = Steps(
        reduce_one(across, k_part, lambda c: k_out.at[:, chunk_of(c, 128)], k_hold, sems_for(7)),
        reduce_one(across, v_part, lambda c: v_out.at[:, chunk_of(c, 128)], v_hold, sems_for(7)),
    )
    last_steps.take()
    normed_grad(core)
    for programs, count in TAIL_PLAN:
        (rows_steps, last_steps, early_steps, weights_steps, out_steps)[programs].take(count)
    rows_steps.finish()

    whole = local_ref[...]
    unit = unit_ref[...]
    scaled = whole * vector(0)
    lane = lax.broadcasted_iota(jnp.int32, (1, 128), 1)
    first = jnp.sum(scaled, axis=1, keepdims=True)
    second = jnp.sum(scaled * unit, axis=1, keepdims=True)
    stats[...] = jnp.where(lane == 0, first, jnp.where(lane == 1, second, 0.0)).T[:8]
    stats_steps = Steps(sum_small(stats, stats_sum, stats_hold, sems_for(2), peers("fsdp")))
    stats_steps.take()
    cotangent = dy_all[core, :, chunk_of(fsdp, width)].astype(F32)
    vec[...] = jnp.zeros_like(vec)
    vec[0:1, :] = jnp.sum(whole * unit, axis=0, keepdims=True)
    vec[1:2, :] = jnp.sum(whole, axis=0, keepdims=True)
    vec[2:3, :] = jnp.sum(cotangent, axis=0, keepdims=True)
    for i in range(3):
        vec[3 + i : 4 + i, chunk_of(core, 128)] = jnp.sum(pre[:, 128 * i : 128 * i + 128].astype(F32), axis=0, keepdims=True)
    for i in range(2):
        vec[pl.ds(6 + 2 * core + i, 1), :] = inner_sum[:, 256 * i : 256 * i + 256]
    vec_steps = Steps(sum_small(vec, vec_out, vec_hold, sems_for(2), peers("ctx")))
    vec_steps.take()
    early_steps.take(9)
    weights_steps.finish()
    out_steps.finish()
    stats_steps.finish()
    back = jnp.concatenate([stats_sum[...], jnp.zeros((120, rows), F32)], axis=0).T * (1.0 / 2048)
    input_out[...] = cotangent + inv_ref[...] * (scaled - back[:, 0:1] - unit * back[:, 1:2])
    vec_steps.finish()
    weights_steps.finish()
    early_steps.finish()
    last_steps.finish()
    assert not sems


def layer(order, ids, x, dy, vectors, weights):
    rows, width = dy.shape
    wide, both = weights[0].shape[0], 2 * rows

    def bf(*shape):
        return pltpu.VMEM(shape, BF16)

    def f32(*shape):
        return pltpu.VMEM(shape, F32)

    def of(kind, *shape):
        return jax.ShapeDtypeStruct(shape, kind)

    return pl.pallas_call(
        layer_kernel,
        out_shape=[
            of(BF16, rows, width),
            of(F32, rows, width),
            of(F32, 16, width),
            of(BF16, wide, width),
            of(BF16, wide, width),
            of(BF16, wide, width),
            of(BF16, 2, 128, wide),
            of(BF16, wide, 1024),
            of(BF16, 2, 512, wide),
        ],
        in_specs=[SMEM, VMEM, ANY, ANY, VMEM] + [ANY] * len(weights),
        out_specs=[VMEM] * 3 + [ANY] * 6,
        scratch_shapes=[
            bf(rows + 16, wide),
            bf(2, rows, wide),
            bf(2, rows, wide),
            bf(wide, 384),
            bf(128, wide),
            bf(wide, 512),
            bf(512, wide),
            bf(GROUPS, GROUP, 256),
            f32(both, 512),
            bf(both, 512),
            bf(512, both),
            bf(both, 512),
            bf(2, rows, wide),
            bf(2, rows, wide),
            bf(wide, 512),
            bf(512, wide),
            bf(128, wide),
            f32(both, 128),
            f32(both, 128),
            bf(4, GROUP, 128),
            bf(4, GROUP, 128),
            pltpu.VMEM((4, 1, TILE), jnp.int32),
            f32(rows, width),
            f32(rows, 1),
            f32(1, 512),
            pltpu.SMEM((GROUPS,), jnp.int32),
            f32(2, STATES, 1, TILE),
            f32(2, STATES, 1, TILE),
            f32(2, STATES, 128, TILE),
            bf(2, ITEMS, 2, GROUP, 256),
            f32(4, 1, TILE),
            f32(4, 1, TILE),
            bf(4, GROUP, 128),
            f32(4, GROUP, 128),
            bf(rows, wide),
            bf(HOLD, rows, width),
            f32(rows, width),
            bf(rows, wide),
            bf(HOLD, rows, width),
            f32(rows, width),
            reduce_scratch((wide, 512)),
            reduce_scratch((512, wide)),
            reduce_scratch((wide, 128)),
            reduce_scratch((wide, 128)),
            reduce_scratch((wide, 128)),
            reduce_scratch((128, wide)),
            bf(HOLD, 4, GROUP, 256),
            f32(4, GROUP, 256),
            bf(both, 384),
            f32(8, rows),
            f32(7, 8, rows),
            f32(8, rows),
            f32(16, width),
            f32(15, 16, width),
        ]
        + pairs(GATHER_SLOTS) * 3
        + pairs(4)
        + [pltpu.SemaphoreType.DMA((8,))]
        + reduce_sems() * 2
        + pairs(1)
        + pairs(SCATTER_SLOTS)
        + reduce_sems()
        + pairs(SCATTER_SLOTS)
        + reduce_sems()
        + pairs(1)
        + pairs(SCATTER_SLOTS)
        + reduce_sems() * 2
        + pairs(7)
        + pairs(15),
        compiler_params=params(0, 63),
        name="layer",
    )(order, ids, x, dy, vectors, *weights)


def body(
    layer_input,
    norm_gain,
    norm_bias,
    query_weight,
    query_bias,
    key_weight,
    key_bias,
    value_weight,
    value_bias,
    out_weight,
    out_bias,
    inner_weight,
    inner_bias,
    outer_weight,
    outer_bias,
    output_grad,
    group_order,
    sequence_ids,
):
    parts = [norm_gain, norm_bias, query_bias, key_bias, value_bias, out_bias, outer_bias, inner_bias]
    ends = [sum(p.shape[0] for p in parts[: i + 1]) for i in range(len(parts))]
    vectors = sum(jnp.pad(p.astype(F32), (end - p.shape[0], ends[-1] - end)) for p, end in zip(parts, ends))
    layer_output, input_grad, vectors, query_grad, key_grad, value_grad, out_grad, inner_w_grad, outer_w_grad = layer(
        group_order,
        sequence_ids.reshape(-1, 128),
        layer_input,
        output_grad,
        vectors[None],
        [query_weight, key_weight, value_weight, out_weight, inner_weight, outer_weight],
    )

    return (
        layer_output,
        input_grad,
        vectors[0],
        vectors[1],
        query_grad.astype(F32),
        vectors[3],
        key_grad.astype(F32),
        vectors[4],
        value_grad.astype(F32),
        vectors[5],
        out_grad.reshape(256, 2048).astype(F32),
        vectors[2],
        inner_w_grad.astype(F32),
        vectors[6:10].reshape(1024),
        outer_w_grad.reshape(1024, 2048).astype(F32),
        vectors[2],
    )


def solution(mesh):
    in_specs = (
        P("ctx", "fsdp"),
        P("fsdp"),
        P("fsdp"),
        P(None, "fsdp"),
        P("fsdp"),
        P(None, "fsdp"),
        P("fsdp"),
        P(None, "fsdp"),
        P("fsdp"),
        P("fsdp", None),
        P("fsdp"),
        P(None, "fsdp"),
        P("fsdp"),
        P("fsdp", None),
        P("fsdp"),
        P("ctx", "fsdp"),
        P(),
        P(),
    )
    out_specs = (
        P("ctx", "fsdp"),
        P("ctx", "fsdp"),
        P("fsdp"),
        P("fsdp"),
        P(None, "fsdp"),
        P("fsdp"),
        P(None, "fsdp"),
        P("fsdp"),
        P(None, "fsdp"),
        P("fsdp"),
        P("fsdp", None),
        P("fsdp"),
        P(None, "fsdp"),
        P("fsdp"),
        P("fsdp", None),
        P("fsdp"),
    )
    return jax.shard_map(body, mesh=mesh, in_specs=in_specs, out_specs=out_specs, check_vma=False)
```

profile of v0, /device:TPU:1, one launch (start us, length us, event | category | flops | bytes accessed | tf_op | source)
XLA Modules:
  0.0 232.8 jit_solution(5218209385315010995)
XLA Ops:
  0.6 0.8 convert_add_fusion
  1.4 0.6 broadcast_in_dim.3.vectors_ref
  2.0 208.5 %layer.1 = (bf16[384,256]{1,0:T(8,128)(2,1)}, f32[384,256]{1,0:T(8,128)}, f32[16,256]{1,0:T(8,128)}, bf16[2048,256]{1,0:T(8,128)(2,1)}, bf16[2048,256]{1,0:T(8,1...) custom-call(s32[32]{0:T(128)} %order_ref.1, ...), custom_call_target="tpu_custom_call" | custom-call | tf_op jit(solution)/shard_map/layer/pallas_call | solution.py:945
  210.6 1.5 fusion
  212.1 0.0 copy-start.7
  212.1 0.7 slice_bitcast_fusion
  212.8 0.6 copy.34
  213.4 6.8 %bitcast_convert_fusion = f32[1024,2048]{1,0:T(8,128)} fusion(bf16[2,512,2048]{2,1,0:T(8,128)(2,1)} %get-tuple-element.33), kind=kLoop, calls=%fused_computation | loop fusion | flops 2097152 | bytes 12582912 | tf_op jit(solution)/shard_map/convert_element_type | solution.py:1082
  220.2 0.0 copy-done
  220.2 4.4 %convert_element_type.53 = f32[2048,1024]{1,0:T(8,128)} convert(bf16[2048,1024]{1,0:T(8,128)(2,1)S(1)} %copy-done) | non-fusion elementwise | flops 2097152 | bytes 12582912 | tf_op jit(solution)/shard_map/convert_element_type | solution.py:1080
  224.7 0.0 copy-done.4
  224.7 1.6 bitcast_convert_fusion.1
  226.3 0.0 copy-done.3
  226.3 1.5 convert_element_type.48
  227.8 0.0 copy-done.2
  227.8 1.5 convert_element_type.49
  229.3 0.0 copy-done.1
  229.3 1.5 convert_element_type.50
  230.8 0.0 copy-done.7
  230.8 0.6 copy.38
  231.3 0.0 copy-done.6
  231.3 0.7 copy.39
  232.0 0.0 copy-done.5
  232.0 0.7 copy.40
  (7 shorter events, 0.0 us)
Async XLA Ops:
  212.1 18.7 %copy-start.7 = (f32[1,256]{1,0:T(1,128)}, f32[1,256]{1,0:T(1,128)S(1)}, u32[]{:S(2)}) copy-start(f32[1,256]{1,0:T(1,128)S(1)} %get-tuple-element.34) | copy-start | bytes 3076
  213.4 6.8 %copy-start = (bf16[2048,1024]{1,0:T(8,128)(2,1)S(1)}, bf16[2048,1024]{1,0:T(8,128)(2,1)}, u32[]{:S(2)}) copy-start(bf16[2048,1024]{1,0:T(8,128)(2,1)} %get-tuple-element.32) | copy-start | bytes 12582916
  220.2 4.4 %copy-start.4 = (bf16[2,128,2048]{2,1,0:T(8,128)(2,1)S(1)}, bf16[2,128,2048]{2,1,0:T(8,128)(2,1)}, u32[]{:S(2)}) copy-start(bf16[2,128,2048]{2,1,0:T(8,128)(2,1)} %get-tuple-element.31) | copy-start | bytes 3145732
  220.2 6.1 %copy-start.3 = (bf16[2048,256]{1,0:T(8,128)(2,1)S(1)}, bf16[2048,256]{1,0:T(8,128)(2,1)}, u32[]{:S(2)}) copy-start(bf16[2048,256]{1,0:T(8,128)(2,1)} %get-tuple-element.28) | copy-start | bytes 3145732
  224.7 3.1 %copy-start.2 = (bf16[2048,256]{1,0:T(8,128)(2,1)S(1)}, bf16[2048,256]{1,0:T(8,128)(2,1)}, u32[]{:S(2)}) copy-start(bf16[2048,256]{1,0:T(8,128)(2,1)} %get-tuple-element.29) | copy-start | bytes 3145732
  224.7 4.6 %copy-start.1 = (bf16[2048,256]{1,0:T(8,128)(2,1)S(1)}, bf16[2048,256]{1,0:T(8,128)(2,1)}, u32[]{:S(2)}) copy-start(bf16[2048,256]{1,0:T(8,128)(2,1)} %get-tuple-element.30) | copy-start | bytes 3145732
  226.3 5.0 %copy-start.6 = (bf16[384,256]{1,0:T(8,128)(2,1)S(1)}, bf16[384,256]{1,0:T(8,128)(2,1)}, u32[]{:S(2)}) copy-start(bf16[384,256]{1,0:T(8,128)(2,1)} %get-tuple-element.88) | copy-start | bytes 589828
  226.3 5.7 %copy-start.5 = (f32[384,256]{1,0:T(8,128)S(1)}, f32[384,256]{1,0:T(8,128)}, u32[]{:S(2)}) copy-start(f32[384,256]{1,0:T(8,128)} %get-tuple-element.89) | copy-start | bytes 1179652
where the time goes:
time: 233 us
  Pallas kernels  209 us (90%)
  other arithmetic  18.1 us (8%)
  local copies, waits for them, and re-layouts  5.45 us (2%)
    pallas_call x1, Pallas kernels, layer(): pl.pallas_call(layer_kernel, out_shape=[of(BF16, rows, width), of(F32, ro...  209 us
    convert_element_type x1, other arithmetic, body(): outer_w_grad.reshape(1024, 2048).astype(F32)  6.8 us

commit v1 on v0

--- a/solution.py
+++ b/solution.py
@@ -95,7 +95,7 @@
 GATHER_SLOTS = len(GATHER)
 
 
-def gather(group, view, sems, arrived=None, own=None):
+def gather(group, view, sems, arrived=None, own=None, halves=False):
     started = []
 
     def start(slot):
@@ -109,8 +109,14 @@
         copy().start()
         started.append(copy)
 
-    for slot in range(GATHER_SLOTS):
-        if GATHER[slot][5] is None:
+    if halves:
+        for slot in (0, 1, 5):
+            start(slot)
+        yield
+        for slot in (2, 3, 4):
+            start(slot)
+    else:
+        for slot in range(6):
             start(slot)
     if arrived:
         arrived((0, 0), 0, 4)
@@ -590,8 +596,10 @@
             kv_all[4 * chip + slot, :, :128] = turned(pre_rows[part_rows, 128:256] + bias[1], cosine, sine).astype(BF16)
             kv_all[4 * chip + slot, :, 128:] = (pre_rows[part_rows, 256:] + bias[2]).astype(BF16)
 
-    def both_cores(one, ref):
+    def both_cores(one, ref, between=None):
         def here():
+            if between:
+                between()
             for i in range(2):
                 exchange(ref, i).wait()
 
@@ -602,12 +610,11 @@
 
         lax.fori_loop(0, 2, loop, 0)
 
-    both_cores(project, normed)
-
     def kv_view(member, a, b):
-        return kv_all.at[pl.ds(4 * member + a, b - a)]
-
-    kv_steps = Steps(gather(across, kv_view, ks))
+        return kv_all.at[pl.ds(4 * member + lax.rem(a + 2 * core, 4), b - a)]
+
+    kv_steps = Steps(gather(across, kv_view, ks, halves=True))
+    both_cores(project, normed, kv_steps.take)
     kv_steps.take()
     dy_steps.take(6)
     copies.wait(5, 6, 7)

time: 233 us -> 234 us (level)
  no operation moved by 1% of the time
where the time goes in v1:
time: 234 us; the launch traced here: 233 us
  Pallas kernels  209 us (89%)
  other arithmetic  18.1 us (8%)
  local copies, waits for them, and re-layouts  5.45 us (2%)
    pallas_call x1, Pallas kernels, layer(): pl.pallas_call(layer_kernel, out_shape=[of(BF16, rows, width), of(F32, ro...  209 us
    convert_element_type x1, other arithmetic, body(): outer_w_grad.reshape(1024, 2048).astype(F32)  6.8 us

profile of v1, /device:TPU:1, one launch (start us, length us, event | category | flops | bytes accessed | tf_op | source)
XLA Modules:
  0.0 233.2 jit_solution(805522012781442216)
XLA Ops:
  0.6 0.8 convert_add_fusion
  1.4 0.6 broadcast_in_dim.3.vectors_ref
  2.0 209.0 %layer.1 = (bf16[384,256]{1,0:T(8,128)(2,1)}, f32[384,256]{1,0:T(8,128)}, f32[16,256]{1,0:T(8,128)}, bf16[2048,256]{1,0:T(8,128)(2,1)}, bf16[2048,256]{1,0:T(8,1...) custom-call(s32[32]{0:T(128)} %order_ref.1, ...), custom_call_target="tpu_custom_call" | custom-call | tf_op jit(solution)/shard_map/layer/pallas_call | solution.py:952
  211.1 1.5 fusion
  212.6 0.0 copy-start.7
  212.6 0.7 slice_bitcast_fusion
  213.3 0.6 copy.34
  213.9 6.8 %bitcast_convert_fusion = f32[1024,2048]{1,0:T(8,128)} fusion(bf16[2,512,2048]{2,1,0:T(8,128)(2,1)} %get-tuple-element.33), kind=kLoop, calls=%fused_computation | loop fusion | flops 2097152 | bytes 12582912 | tf_op jit(solution)/shard_map/convert_element_type | solution.py:1089
  220.7 0.0 copy-done
  220.7 4.4 %convert_element_type.53 = f32[2048,1024]{1,0:T(8,128)} convert(bf16[2048,1024]{1,0:T(8,128)(2,1)S(1)} %copy-done) | non-fusion elementwise | flops 2097152 | bytes 12582912 | tf_op jit(solution)/shard_map/convert_element_type | solution.py:1087
  225.1 0.0 copy-done.4
  225.1 1.6 bitcast_convert_fusion.1
  226.8 0.0 copy-done.3
  226.8 1.5 convert_element_type.48
  228.3 0.0 copy-done.2
  228.3 1.5 convert_element_type.49
  229.7 0.0 copy-done.1
  229.7 1.5 convert_element_type.50
  231.2 0.0 copy-done.7
  231.2 0.6 copy.38
  231.8 0.0 copy-done.6
  231.8 0.7 copy.39
  232.5 0.0 copy-done.5
  232.5 0.7 copy.40
  (7 shorter events, 0.0 us)
Async XLA Ops:
  212.6 18.7 %copy-start.7 = (f32[1,256]{1,0:T(1,128)}, f32[1,256]{1,0:T(1,128)S(1)}, u32[]{:S(2)}) copy-start(f32[1,256]{1,0:T(1,128)S(1)} %get-tuple-element.34) | copy-start | bytes 3076
  213.9 6.8 %copy-start = (bf16[2048,1024]{1,0:T(8,128)(2,1)S(1)}, bf16[2048,1024]{1,0:T(8,128)(2,1)}, u32[]{:S(2)}) copy-start(bf16[2048,1024]{1,0:T(8,128)(2,1)} %get-tuple-element.32) | copy-start | bytes 12582916
  220.7 4.4 %copy-start.4 = (bf16[2,128,2048]{2,1,0:T(8,128)(2,1)S(1)}, bf16[2,128,2048]{2,1,0:T(8,128)(2,1)}, u32[]{:S(2)}) copy-start(bf16[2,128,2048]{2,1,0:T(8,128)(2,1)} %get-tuple-element.31) | copy-start | bytes 3145732
  220.7 6.1 %copy-start.3 = (bf16[2048,256]{1,0:T(8,128)(2,1)S(1)}, bf16[2048,256]{1,0:T(8,128)(2,1)}, u32[]{:S(2)}) copy-start(bf16[2048,256]{1,0:T(8,128)(2,1)} %get-tuple-element.28) | copy-start | bytes 3145732
  225.1 3.1 %copy-start.2 = (bf16[2048,256]{1,0:T(8,128)(2,1)S(1)}, bf16[2048,256]{1,0:T(8,128)(2,1)}, u32[]{:S(2)}) copy-start(bf16[2048,256]{1,0:T(8,128)(2,1)} %get-tuple-element.29) | copy-start | bytes 3145732
  225.1 4.6 %copy-start.1 = (bf16[2048,256]{1,0:T(8,128)(2,1)S(1)}, bf16[2048,256]{1,0:T(8,128)(2,1)}, u32[]{:S(2)}) copy-start(bf16[2048,256]{1,0:T(8,128)(2,1)} %get-tuple-element.30) | copy-start | bytes 3145732
  226.8 5.0 %copy-start.6 = (bf16[384,256]{1,0:T(8,128)(2,1)S(1)}, bf16[384,256]{1,0:T(8,128)(2,1)}, u32[]{:S(2)}) copy-start(bf16[384,256]{1,0:T(8,128)(2,1)} %get-tuple-element.88) | copy-start | bytes 589828
  226.8 5.7 %copy-start.5 = (f32[384,256]{1,0:T(8,128)S(1)}, f32[384,256]{1,0:T(8,128)}, u32[]{:S(2)}) copy-start(f32[384,256]{1,0:T(8,128)} %get-tuple-element.89) | copy-start | bytes 1179652
